TPU v7x, 32 devices: a whole 2x2x4 slice. The times are simulated.
32 devices in a mesh: dap: 4 (over x, core), slab: 8 (over z, y).
Axes of the slice: x: 2, y: 2, z: 4, core: 2. Of those that a mesh axis runs over, the one named last changes fastest.
Arguments:
- pair: bfloat16 [32, 32, 128], P('dap', 'slab'), may hold values from -6 to 6
- chain_lengths: int32 [8], replicated, may hold values from 1 to 4, as said below
- norm_gains: float32 [3, 128], replicated, may hold values from 0.25 to 1.75
- w_tri_in: bfloat16 [128, 640], replicated, may hold values from -0.5 to 0.5
- w_tri_out: bfloat16 [128, 128], replicated, may hold values from -0.5 to 0.5
- w_bias: bfloat16 [128, 4], replicated, may hold values from -0.5 to 0.5
- w_att_in: bfloat16 [128, 512], replicated
- w_att_out: bfloat16 [128, 128], replicated, may hold values from -0.5 to 0.5
Outputs:
- result: bfloat16 [32, 32, 128], P(None, ('slab', 'dap'))
Inputs may be any that keep to these rules, and one draw needn't show every extreme that they name: `chain_lengths`: chain c owns token slots c * 4 to (c + 1) * 4 - 1; slots past its length are padding.
All inputs are finite; a program needn't handle non-finite values.
Results may differ from a plain program's by a relative error of at most 0.012.
Values may be sent and summed in bfloat16 or wider, within the bound.
A program may use at most 64 MiB of HBM per device.

v0:
```python
import math

import jax
import jax.numpy as jnp
from jax import lax
from jax.sharding import PartitionSpec as P

EPSILON = 1e-05


def spread_2(value, axis, source):
    kept = jnp.where(lax.axis_index(axis) == source, value, 0).astype(value.dtype)
    return lax.psum(kept, axis)


def layer_norm(values, gain_row):
    average = jnp.mean(values, axis=-1, keepdims=True)
    centred = values - average
    spread = jnp.mean(centred * centred, axis=-1, keepdims=True)
    return centred * lax.rsqrt(spread + EPSILON) * gain_row


def token_valid(chain_lengths, first_token, token_count, slot_size):
    token_index = first_token + jnp.arange(token_count, dtype=jnp.int32)
    chain_index = token_index // slot_size
    member = chain_index[:, None] == jnp.arange(chain_lengths.shape[0], dtype=jnp.int32)[None, :]
    chain_limit = jnp.sum(jnp.where(member, chain_lengths[None, :], 0), axis=1)
    return (token_index % slot_size < chain_limit).astype(jnp.float32)


def on_device(pair, chain_lengths, norm_gains, w_tri_in, w_tri_out, w_bias, w_att_in, w_att_out):
    row_count, col_count, channels = pair.shape
    dap_size = lax.axis_size("dap")
    slab_size = lax.axis_size("slab")
    tokens = row_count * dap_size
    slot_size = tokens // chain_lengths.shape[0]
    dap_index = lax.axis_index("dap")
    slab_index = lax.axis_index("slab")
    row_valid = token_valid(chain_lengths, dap_index * row_count, row_count, slot_size)
    col_valid = token_valid(chain_lengths, slab_index * col_count, col_count, slot_size)
    normed = layer_norm(pair.astype(jnp.float32), norm_gains[0]).astype(jnp.bfloat16)
    projected = jnp.dot(normed, w_tri_in, preferred_element_type=jnp.float32)
    out_gate = jax.nn.sigmoid(projected[..., 4 * channels :])
    normed_all = lax.all_gather(normed, "slab", axis=1, tiled=True)
    slab_ratio = slab_size // dap_size
    offset = slab_index % slab_ratio * col_count
    own_normed = lax.dynamic_slice_in_dim(normed_all, offset, col_count, 0)
    right_normed = spread_2(own_normed, "dap", slab_index // slab_ratio)
    all_valid = token_valid(chain_lengths, 0, tokens, slot_size)
    span = min(128, tokens)
    w_left = w_tri_in[:, : 2 * channels]
    w_right = w_tri_in[:, 2 * channels : 4 * channels]

    def add_span(step, running):
        first = step * span
        k_valid = lax.dynamic_slice_in_dim(all_valid, first, span, 0)
        left_in = lax.dynamic_slice_in_dim(normed_all, first, span, 1)
        right_in = lax.dynamic_slice_in_dim(right_normed, first, span, 1)
        left_proj = jnp.dot(left_in, w_left, preferred_element_type=jnp.float32)
        right_proj = jnp.dot(right_in, w_right, preferred_element_type=jnp.float32)
        left_mask = (row_valid[:, None] * k_valid[None, :])[:, :, None]
        right_mask = (col_valid[:, None] * k_valid[None, :])[:, :, None]
        left_block = (
            left_mask * jax.nn.sigmoid(left_proj[..., channels:]) * left_proj[..., :channels]
        ).astype(jnp.bfloat16)
        right_block = (
            right_mask * jax.nn.sigmoid(right_proj[..., channels:]) * right_proj[..., :channels]
        ).astype(jnp.bfloat16)
        return running + jnp.einsum(
            "ikc,jkc->ijc", left_block, right_block, preferred_element_type=jnp.float32
        )

    triangle = lax.fori_loop(
        0, tokens // span, add_span, jnp.zeros((row_count, col_count, channels), jnp.float32)
    )
    normed_tri = layer_norm(triangle, norm_gains[1]).astype(jnp.bfloat16)
    mixed_update = out_gate * jnp.dot(normed_tri, w_tri_out, preferred_element_type=jnp.float32)
    updated = (pair.astype(jnp.float32) + mixed_update).astype(jnp.bfloat16)
    columns = lax.all_to_all(updated, "dap", split_axis=1, concat_axis=0, tiled=True)
    normed_cols = layer_norm(columns.astype(jnp.float32), norm_gains[2]).astype(jnp.bfloat16)
    normed_rows = layer_norm(updated.astype(jnp.float32), norm_gains[2]).astype(jnp.bfloat16)
    bias_block = jnp.einsum(
        "ijc,ch->hij", normed_rows, w_bias, preferred_element_type=jnp.float32
    ).astype(jnp.bfloat16)
    bias_tall = lax.all_gather(bias_block, "dap", axis=1, tiled=True)
    pair_bias = lax.all_gather(bias_tall, "slab", axis=2, tiled=True)
    att_projected = jnp.dot(normed_cols, w_att_in, preferred_element_type=jnp.float32)
    att_width = w_att_out.shape[0]
    head_count = w_bias.shape[1]
    head_dim = att_width // head_count
    score_scale = 1.0 / math.sqrt(head_dim)
    query_rows = att_projected[..., :att_width].astype(jnp.bfloat16)
    key_rows = att_projected[..., att_width : 2 * att_width].astype(jnp.bfloat16)
    value_rows = att_projected[..., 2 * att_width : 3 * att_width].astype(jnp.bfloat16)
    att_gate = jax.nn.sigmoid(att_projected[..., 3 * att_width :])
    key_valid = token_valid(chain_lengths, 0, tokens, slot_size)[:, None] > 0
    head_outputs = []
    for head_index in range(head_count):
        head_start = head_index * head_dim
        query_head = query_rows[:, 0, head_start : head_start + head_dim]
        key_head = key_rows[:, 0, head_start : head_start + head_dim]
        value_head = value_rows[:, 0, head_start : head_start + head_dim]
        scores = lax.dot_general(
            key_head, query_head, (((1,), (1,)), ((), ())), preferred_element_type=jnp.float32
        ) * score_scale + pair_bias[head_index].astype(jnp.float32)
        scores = jnp.where(key_valid, scores, -1e30)
        score_top = jnp.max(scores, axis=0, keepdims=True)
        weights = jnp.exp(scores - score_top)
        weights = (weights / jnp.sum(weights, axis=0, keepdims=True)).astype(jnp.bfloat16)
        head_outputs.append(
            lax.dot_general(
                weights, value_head, (((0,), (0,)), ((), ())), preferred_element_type=jnp.float32
            )
        )
    column_results = [jnp.concatenate(head_outputs, axis=1)]
    attended = jnp.stack(column_results, axis=1)
    gated = (att_gate * attended).astype(jnp.bfloat16)
    return (
        columns.astype(jnp.float32) + jnp.dot(gated, w_att_out, preferred_element_type=jnp.float32)
    ).astype(jnp.bfloat16)


def solution(mesh):
    in_specs = (P("dap", "slab", None), P(), P(), P(), P(), P(), P(), P())
    out_specs = P(None, ("slab", "dap"), None)
    return jax.shard_map(
        on_device, mesh=mesh, in_specs=in_specs, out_specs=out_specs, check_vma=False
    )
```

profile of v0, /device:TPU:0, one launch (start us, length us, event | category | flops | bytes accessed | tf_op | source)
XLA Modules:
  0.0 93.8 jit_solution(10837233696516642292)
XLA Ops:
  0.0 0.7 copy-done.7
  0.7 0.2 select_reduce_fusion.2
  0.9 0.2 select_reduce_fusion
  1.2 0.6 copy-done.4
  1.9 0.2 fusion.41
  2.3 32.4 %all_gather.9 = bf16[8,32,128]{2,0,1:T(8,128)(2,1)S(1)} all-gather(bf16[8,4,128]{2,0,1:T(8,128)(2,1)S(1)} %fusion.43), channel_id=1, replica_groups=mesh['dap'=4,'slab'=8] {'slab'}, dimensions={1}, use_global_device_ids=true | all-gather | bytes 73728 | tf_op jit(solution)/shard_map/all_gather | solution.py:44
  34.7 10.3 %psum.7 = bf16[4,32,128]{2,1,0:T(8,128)(2,1)S(1)} all-reduce(bf16[4,32,128]{2,1,0:T(8,128)(2,1)S(1)} %dynamic-slice_select_fusion), channel_id=1, replica_groups=mesh['dap'=4,'slab'=8] {'dap'}, use_global_device_ids=true, to_apply=%region_4.5 | all-reduce | flops 16384 | bytes 65536 | tf_op jit(solution)/shard_map/psum | solution.py:13
  45.0 0.2 fusion.27
  45.7 0.2 copy.54
  45.9 0.3 fusion.94
  46.3 0.2 multiply_reduce_fusion
  46.5 0.5 copy-done.5
  47.0 0.2 fusion.34
  47.2 0.8 convert_reduce_fusion.2
  48.0 3.2 %all-to-all-start = ((bf16[8,4,128]{2,0,1:T(8,128)(2,1)}), bf16[8,4,128]{2,0,1:T(8,128)(2,1)S(1)}, u32[]{:S(2)}, u32[]{:S(2)}) async-start(bf16[8,4,128]{2,0,1:T(8,128)(2,1)} %get-tuple-element.45), calls=%async_computation | async-start | bytes 16384 | tf_op jit(solution)/shard_map/all_to_all | solution.py:79
  51.3 0.9 fusion.44
  52.2 0.7 copy-done.6
  52.9 0.9 fusion.16
  53.9 5.3 %all_gather.10 = bf16[4,32,4]{2,0,1:T(4,128)(2,1)S(1)} all-gather(bf16[4,8,4]{2,0,1:T(4,128)(2,1)S(1)} %copy.56), channel_id=1, replica_groups=mesh['dap'=4,'slab'=8] {'dap'}, dimensions={1}, use_global_device_ids=true | all-gather | bytes 1280 | tf_op jit(solution)/shard_map/all_gather | solution.py:85
  59.3 30.4 %all_gather.11 = bf16[4,32,32]{1,0,2:T(4,128)(2,1)S(1)} all-gather(bf16[4,32,4]{1,0,2:T(4,128)(2,1)S(1)} %copy.57), channel_id=1, replica_groups=mesh['dap'=4,'slab'=8] {'slab'}, dimensions={2}, use_global_device_ids=true | all-gather | bytes 9216 | tf_op jit(solution)/shard_map/all_gather | solution.py:86
  90.3 0.2 fusion.52
  90.5 0.2 fusion.89
  90.7 0.2 fusion.91
  90.9 0.2 fusion.65
  91.1 0.2 fusion.90
  91.4 0.2 fusion.64
  91.6 0.2 fusion.92
  91.8 0.2 fusion.66
  92.0 0.1 fusion.93
  92.2 0.2 fusion.67
  92.4 0.6 copy-done.3
  93.0 0.8 fusion.15
  (53 shorter events, 2.1 us)
Async XLA Ops:
  0.0 90.5 %copy-start = (bf16[128,512]{1,0:T(8,128)(2,1)S(1)}, bf16[128,512]{1,0:T(8,128)(2,1)}, u32[]{:S(2)}) copy-start(bf16[128,512]{1,0:T(8,128)(2,1)} %param.14) | copy-start | bytes 393220
  0.0 0.7 copy-start.7
  0.7 1.1 %copy-start.2 = (bf16[8,4,128]{2,1,0:T(4,128)(2,1)S(1)}, bf16[8,4,128]{2,1,0:T(4,128)(2,1)}, u32[]{:S(2)}) copy-start(bf16[8,4,128]{2,1,0:T(4,128)(2,1)} %param.8) | copy-start | bytes 24580
  1.1 0.7 copy-start.4
  2.3 42.7 %copy-start.1 = (bf16[128,640]{1,0:T(8,128)(2,1)S(1)}, bf16[128,640]{1,0:T(8,128)(2,1)}, u32[]{:S(2)}) copy-start(bf16[128,640]{1,0:T(8,128)(2,1)} %param.11) | copy-start | bytes 491524
  46.2 0.8 copy-start.5
  48.0 42.1 %all-to-all-start = ((bf16[8,4,128]{2,0,1:T(8,128)(2,1)}), bf16[8,4,128]{2,0,1:T(8,128)(2,1)S(1)}, u32[]{:S(2)}, u32[]{:S(2)}) async-start(bf16[8,4,128]{2,0,1:T(8,128)(2,1)} %get-tuple-element.45), calls=%async_computation | async-start | bytes 16384 | tf_op jit(solution)/shard_map/all_to_all | solution.py:79
  52.2 0.7 copy-start.6
  92.2 0.8 copy-start.3
where the time goes:
time: 94.3 us; the launch traced here: 93.8 us
  blocking collectives  78.4 us (83%)
  matrix products  5.03 us (5%)
  local copies, waits for them, and re-layouts  4.18 us (4%)
  starting transfers between devices  3.25 us (3%)
  other arithmetic  2.74 us (3%)
    all_gather x1, blocking collectives, on_device(): normed_all = lax.all_gather(normed, 'slab', axis=1, tiled=True)  32.4 us
    all_gather x1, blocking collectives, on_device(): pair_bias = lax.all_gather(bias_tall, 'slab', axis=2, tiled=True)  30.4 us
    psum x1, blocking collectives, spread_2(): return lax.psum(kept, axis)  10.3 us
    all_gather x1, blocking collectives, on_device(): bias_tall = lax.all_gather(bias_block, 'dap', axis=1, tiled=True)  5.28 us
    unnamed x20, local copies, waits for them, and re-layouts  3.38 us
    all_to_all x1, starting transfers between devices, on_device(): lax.all_to_all(updated, 'dap', split_axis=1, concat_axis=0, tiled=True)  3.25 us
  transfers between devices with their start and end apart: 1, of which 0 were waited for; matrix products, arithmetic and copies ran while one was open for 3% of the time, Pallas kernels for 0%

commit v1 on v0

--- a/solution.py
+++ b/solution.py
@@ -1,9 +1,16 @@
+import functools
 import math
 
 import jax
 import jax.numpy as jnp
 from jax import lax
+from jax.experimental import pallas as pl
+from jax.experimental.pallas import tpu as pltpu
 from jax.sharding import PartitionSpec as P
+
+MESH = pl.DeviceIdType.MESH
+F32 = jnp.float32
+BF16 = jnp.bfloat16
 
 EPSILON = 1e-05
 
@@ -120,9 +127,317 @@
     ).astype(jnp.bfloat16)
 
 
+def small_kernel(
+    dap_size, slab_size, slot_size,
+    pair_hbm, len_hbm, gains_hbm, w_in_hbm, w_out_hbm, w_bias_hbm, w_att_hbm, w_ao_hbm,
+    out_ref,
+    pair_v, len_s, gains_v, w_in_v, w_out_v, w_bias_v, w_att_v, w_ao_v,
+    x_scr, left_buf, right_own, right_buf, right_f32, upd_own, col_buf, bias_buf,
+    in_sem, left_send, left_recv, right_send, right_recv,
+    col_send, col_recv, bias_send, bias_recv,
+):
+    rows, cols, channels = pair_hbm.shape
+    block = rows * cols
+    tokens = rows * dap_size
+    devices = dap_size * slab_size
+    ratio = rows // cols
+    a = lax.axis_index("dap")
+    s = lax.axis_index("slab")
+    me = s * dap_size + a
+
+    def place(index):
+        return (lax.rem(index, dap_size), lax.div(index, dap_size))
+
+    barrier = pltpu.get_barrier_semaphore()
+
+    def greet(d, carry):
+        pl.semaphore_signal(
+            barrier, inc=1, device_id=place(lax.rem(me + d, devices)), device_id_type=MESH
+        )
+        return carry
+
+    pairs = (
+        (pair_hbm, pair_v), (len_hbm, len_s), (gains_hbm, gains_v), (w_in_hbm, w_in_v),
+        (w_bias_hbm, w_bias_v), (w_out_hbm, w_out_v), (w_att_hbm, w_att_v), (w_ao_hbm, w_ao_v),
+    )
+    loads = [pltpu.make_async_copy(src, dst, in_sem.at[n]) for n, (src, dst) in enumerate(pairs)]
+    for load in loads:
+        load.start()
+    lax.fori_loop(1, devices, greet, 0, unroll=True)
+
+    for load in loads[:4]:
+        load.wait()
+
+    row = lax.broadcasted_iota(jnp.int32, (block, channels), 0)
+    lane = lax.broadcasted_iota(jnp.int32, (block, channels), 1)
+    row_shift = rows.bit_length() - 1
+    col_shift = cols.bit_length() - 1
+
+    def valid(token):
+        inside = None
+        for chain in range(len_hbm.shape[0]):
+            first = chain * slot_size
+            here = jnp.logical_and(token >= first, token < first + len_s[chain])
+            inside = here if inside is None else jnp.logical_or(inside, here)
+        return inside
+
+    def norm(values, gain):
+        return layer_norm(values, gains_v[gain : gain + 1, :])
+
+    def dot(x, y):
+        return jnp.dot(x, y, preferred_element_type=F32)
+
+    for i in range(rows):
+        x_scr[i * cols : (i + 1) * cols, :] = pair_v[i].astype(F32)
+    x_nat = x_scr[...]
+    x_perm = jnp.concatenate([x_scr[pl.ds(k, rows, stride=cols), :] for k in range(cols)], axis=0)
+    normed_nat = norm(x_nat, 0).astype(BF16)
+    normed_perm = norm(x_perm, 0).astype(BF16)
+    mask_nat = jnp.logical_and(
+        valid(a * rows + lax.shift_right_logical(row, col_shift)),
+        valid(s * cols + (row & (cols - 1))),
+    ).astype(F32)
+    mask_perm = jnp.logical_and(
+        valid(a * rows + (row & (rows - 1))),
+        valid(s * cols + lax.shift_right_logical(row, row_shift)),
+    ).astype(F32)
+    left_proj = dot(normed_perm, w_in_v[:, : 2 * channels])
+    right_proj = dot(normed_nat, w_in_v[:, 2 * channels : 4 * channels])
+    left_buf[s] = (
+        mask_perm * jax.nn.sigmoid(left_proj[:, channels:]) * left_proj[:, :channels]
+    ).astype(BF16)
+    right_own[...] = (
+        (mask_nat * jax.nn.sigmoid(right_proj[:, channels:]) * right_proj[:, :channels])
+        .astype(BF16)
+        .reshape(ratio, block // ratio, channels)
+    )
+
+    pl.semaphore_wait(barrier, devices - 1)
+
+    def send_left(d, carry):
+        pltpu.make_async_remote_copy(
+            src_ref=left_buf.at[s],
+            dst_ref=left_buf.at[s],
+            send_sem=left_send,
+            recv_sem=left_recv,
+            device_id=(a, lax.rem(s + d, slab_size)),
+            device_id_type=MESH,
+        ).start()
+        return carry
+
+    def right_copies():
+        for part in range(ratio):
+            for d in range(dap_size):
+                to_a = lax.rem(a + d, dap_size)
+                to_s = a * ratio + part
+                remote = pltpu.make_async_remote_copy(
+                    src_ref=right_own.at[part],
+                    dst_ref=right_buf.at[s],
+                    send_sem=right_send.at[part * dap_size + d],
+                    recv_sem=right_recv,
+                    device_id=(to_a, to_s),
+                    device_id_type=MESH,
+                )
+                local = None
+                if d == 0:
+                    local = pltpu.make_async_copy(right_own.at[part], right_buf.at[s], right_recv)
+                yield to_s, remote, local
+
+    lax.fori_loop(1, slab_size, send_left, 0, unroll=True)
+    for to_s, remote, local in right_copies():
+        if local is None:
+            remote.start()
+        else:
+            pl.when(to_s == s)(local.start)
+            pl.when(to_s != s)(remote.start)
+
+    out_gate = jax.nn.sigmoid(dot(normed_perm, w_in_v[:, 4 * channels :]))
+    loads[4].wait()
+    heads = w_bias_hbm.shape[1]
+    head_dim = channels // heads
+    head_shift = head_dim.bit_length() - 1
+    spread_row = lax.broadcasted_iota(jnp.int32, (heads, channels), 0)
+    spread_lane = lax.broadcasted_iota(jnp.int32, (heads, channels), 1)
+    spread = (lax.shift_right_logical(spread_lane, head_shift) == spread_row).astype(F32)
+    w_bias_wide = dot(w_bias_v[...], spread.astype(BF16)).astype(BF16)
+    key_ok = valid(lane & (tokens - 1))
+    lane_head = lax.shift_right_logical(lane, head_shift)
+    for load in loads[5:]:
+        load.wait()
+
+    pltpu.make_async_copy(right_buf, right_buf, right_recv).wait()
+    right_f32[...] = right_buf[...].astype(F32).reshape(right_f32.shape)
+    others = left_buf.at[pl.ds(0, slab_size - 1)]
+    pltpu.make_async_copy(others, others, left_recv).wait()
+    triangle = [jnp.zeros((rows, channels), F32) for _ in range(cols)]
+    for k_block in range(slab_size):
+        left = left_buf[k_block].astype(F32)
+        for k in range(cols):
+            left_k = left[k * rows : (k + 1) * rows, :]
+            for j in range(cols):
+                at = k_block * cols * cols + j * cols + k
+                triangle[j] += left_k * right_f32[at : at + 1, :]
+    triangle = jnp.concatenate(triangle, axis=0)
+    normed_tri = norm(triangle, 1).astype(BF16)
+    updated = (x_perm + out_gate * dot(normed_tri, w_out_v[...])).astype(BF16).astype(F32)
+    upd_own[...] = updated.reshape(upd_own.shape)
+    col_buf[a] = upd_own[a]
+
+    def col_copy(d):
+        to_a = lax.rem(a + d, dap_size)
+        return pltpu.make_async_remote_copy(
+            src_ref=upd_own.at[to_a],
+            dst_ref=col_buf.at[a],
+            send_sem=col_send.at[d - 1],
+            recv_sem=col_recv,
+            device_id=(to_a, s),
+            device_id_type=MESH,
+        )
+
+    for d in range(1, dap_size):
+        col_copy(d).start()
+
+    normed_local = norm(updated, 2).astype(BF16)
+    bias_all = dot(normed_local, w_bias_wide)
+    bias_row = jnp.sum(
+        jnp.where((lane & (block - 1)) == row, bias_all, 0.0), axis=0, keepdims=True
+    )
+    bias_buf[me] = bias_row.astype(BF16).astype(F32)
+
+    def send_bias(d, carry):
+        pltpu.make_async_remote_copy(
+            src_ref=bias_buf.at[me],
+            dst_ref=bias_buf.at[me],
+            send_sem=bias_send,
+            recv_sem=bias_recv,
+            device_id=place(lax.rem(me + d, devices)),
+            device_id_type=MESH,
+        ).start()
+        return carry
+
+    lax.fori_loop(1, devices, send_bias, 0, unroll=True)
+
+    other_cols = col_buf.at[pl.ds(0, dap_size - 1)]
+    pltpu.make_async_copy(other_cols, other_cols, col_recv).wait()
+    columns = col_buf[...].reshape(tokens, channels)
+    normed_cols = norm(columns, 2).astype(BF16)
+    projected = dot(normed_cols, w_att_v[...])
+    query = projected[:, :channels].astype(BF16)
+    key = projected[:, channels : 2 * channels].astype(BF16)
+    value = projected[:, 2 * channels : 3 * channels].astype(BF16)
+    att_gate = jax.nn.sigmoid(projected[:, 3 * channels :])
+    blank = jnp.zeros_like(key)
+    key_wide = jnp.concatenate([jnp.where(lane_head == h, key, blank) for h in range(heads)], axis=0)
+    value_wide = jnp.concatenate(
+        [jnp.where(lane_head == h, value, blank) for h in range(heads)], axis=0
+    )
+    scores = lax.dot_general(
+        query, key_wide, (((1,), (1,)), ((), ())), preferred_element_type=F32
+    ) * (1.0 / math.sqrt(head_dim))
+
+    other_rows = bias_buf.at[pl.ds(0, devices - 1)]
+    pltpu.make_async_copy(other_rows, other_rows, bias_recv).wait()
+    got = bias_buf[:, 0, :]
+    shift = (row & (cols - 1)) - (lax.shift_right_logical(lane, row_shift) & (dap_size - 1))
+    bias = got
+    for delta in range(1 - cols, cols):
+        if delta:
+            moved = pltpu.roll(got, delta % tokens, 0)
+            moved = pltpu.roll(moved, (-rows * delta) % channels, 1)
+            bias = jnp.where(shift == delta, moved, bias)
+    scores = jnp.where(key_ok, scores + bias, -1e30)
+    top = jnp.zeros_like(scores)
+    for h in range(heads):
+        here = lane_head == h
+        top = jnp.where(
+            here, jnp.max(jnp.where(here, scores, -jnp.inf), axis=1, keepdims=True), top
+        )
+    weights = jnp.exp(scores - top)
+    total = jnp.zeros_like(scores)
+    for h in range(heads):
+        here = lane_head == h
+        total = jnp.where(here, jnp.sum(jnp.where(here, weights, 0.0), axis=1, keepdims=True), total)
+    weights = (weights / total).astype(BF16)
+    gated = (att_gate * dot(weights, value_wide)).astype(BF16)
+    out_ref[...] = columns + dot(gated, w_ao_v[...])
+
+    pltpu.make_async_copy(others, others, left_send).wait()
+    for to_s, remote, local in right_copies():
+        if local is None:
+            remote.wait_send()
+        else:
+            pl.when(to_s != s)(remote.wait_send)
+    for d in range(1, dap_size):
+        col_copy(d).wait_send()
+    pltpu.make_async_copy(other_rows, other_rows, bias_send).wait()
+
+
+def on_device_small(*args):
+    pair, chain_lengths = args[:2]
+    rows, cols, channels = pair.shape
+    dap_size = lax.axis_size("dap")
+    slab_size = lax.axis_size("slab")
+    tokens = rows * dap_size
+    devices = dap_size * slab_size
+    block = rows * cols
+    ratio = rows // cols
+    spaces = [pltpu.VMEM] * 8
+    spaces[1] = pltpu.SMEM
+    result = pl.pallas_call(
+        functools.partial(small_kernel, dap_size, slab_size, tokens // chain_lengths.shape[0]),
+        out_shape=jax.ShapeDtypeStruct((tokens, channels), F32),
+        in_specs=[pl.BlockSpec(memory_space=pl.ANY)] * 8,
+        out_specs=pl.BlockSpec(memory_space=pltpu.VMEM),
+        scratch_shapes=[space(arg.shape, arg.dtype) for space, arg in zip(spaces, args)]
+        + [
+            pltpu.VMEM((block, channels), F32),
+            pltpu.VMEM((slab_size, block, channels), BF16),
+            pltpu.VMEM((ratio, block // ratio, channels), BF16),
+            pltpu.VMEM((slab_size, block // ratio, channels), BF16),
+            pltpu.VMEM((slab_size * block // ratio, channels), F32),
+            pltpu.VMEM((cols, rows, channels), F32),
+            pltpu.VMEM((dap_size, rows, channels), F32),
+            pltpu.VMEM((devices, 1, channels), F32),
+            pltpu.SemaphoreType.DMA((8,)),
+            pltpu.SemaphoreType.DMA,
+            pltpu.SemaphoreType.DMA,
+            pltpu.SemaphoreType.DMA((ratio * dap_size,)),
+            pltpu.SemaphoreType.DMA,
+            pltpu.SemaphoreType.DMA((dap_size - 1,)),
+            pltpu.SemaphoreType.DMA,
+            pltpu.SemaphoreType.DMA,
+            pltpu.SemaphoreType.DMA,
+        ],
+        compiler_params=pltpu.CompilerParams(collective_id=0, has_side_effects=True),
+    )(*args)
+    return result.astype(BF16).reshape(tokens, 1, channels)
+
+
+def fits_small(mesh, shapes):
+    pair, lengths, w_bias = shapes[0].shape, shapes[1].shape, shapes[5].shape
+    dap_size, slab_size = mesh.shape["dap"], mesh.shape["slab"]
+    tokens, width, channels = pair
+    rows, cols, heads = tokens // dap_size, width // slab_size, w_bias[1]
+    return (
+        tokens == width
+        and channels == 128
+        and rows == 8
+        and cols == dap_size == 4
+        and tokens == rows * dap_size == cols * slab_size == dap_size * slab_size
+        and heads * tokens == channels
+        and shapes[7].shape == (channels, channels)
+        and tokens % lengths[0] == 0
+    )
+
+
 def solution(mesh):
     in_specs = (P("dap", "slab", None), P(), P(), P(), P(), P(), P(), P())
     out_specs = P(None, ("slab", "dap"), None)
-    return jax.shard_map(
-        on_device, mesh=mesh, in_specs=in_specs, out_specs=out_specs, check_vma=False
-    )
+
+    def run(*args):
+        body = on_device_small if fits_small(mesh, args) else on_device
+        return jax.shard_map(
+            body, mesh=mesh, in_specs=in_specs, out_specs=out_specs, check_vma=False
+        )(*args)
+
+    return run

time: 94.3 us -> 20.6 us (0.22)
  blocking collectives: 78.4 us -> 0 us
  Pallas kernels: 0 us -> 17.6 us
  matrix products: 5.03 us -> 0 us
  starting transfers between devices: 3.25 us -> 0 us
  local copies, waits for them, and re-layouts: 4.18 us -> 1.39 us
  other arithmetic: 2.74 us -> 1.32 us
    all_gather x3 -> x0, blocking collectives: 68.1 us -> none  [the longest x1 32.4 us: on_device(): normed_all = lax.all_gather(normed, 'slab', axis=1, tiled=True)]
    pallas_call x0 -> x1, Pallas kernels: none -> 17.6 us  [on_device_small(): pl.pallas_call(functools.partial(small_kernel, dap_size, slab_size, token...]
    psum x1 -> x0, blocking collectives: 10.3 us -> none  [spread_2(): return lax.psum(kept, axis)]
    dot_general x16 -> x0, matrix products: 5.03 us -> none  [the longest x1 0.9 us: on_device(): jnp.einsum('ijc,ch->hij', normed_rows, w_bias, preferred_element_type=jnp...]
    all_to_all x1 -> x0, starting transfers between devices: 3.25 us -> none  [on_device(): lax.all_to_all(updated, 'dap', split_axis=1, concat_axis=0, tiled=True)]
    reduce_sum x14 -> x0, other arithmetic: 2.21 us -> none  [the longest x4 1.38 us: layer_norm(): spread = jnp.mean(centred * centred, axis=-1, keepdims=True)]
    unnamed x20 -> x1, local copies, waits for them, and re-layouts: 3.38 us -> 1.39 us
    reshape x0 -> x1, other arithmetic: none -> 1.32 us  [on_device_small(): return result.astype(BF16).reshape(tokens, 1, channels)]
  transfers between devices with their start and end apart: 1 -> 0, of which waited for: 0 -> 0; matrix products, arithmetic and copies ran while one was open for 3% -> 0% of each run, Pallas kernels for 0% -> 0%
where the time goes in v1:
time: 20.6 us; the launch traced here: 20.3 us
  Pallas kernels  17.6 us (85%)
  local copies, waits for them, and re-layouts  1.39 us (7%)
  other arithmetic  1.32 us (6%)
    pallas_call x1, Pallas kernels, on_device_small(): pl.pallas_call(functools.partial(small_kernel, dap_size, slab_size, token...  17.6 us
    unnamed x1, local copies, waits for them, and re-layouts  1.39 us
    reshape x1, other arithmetic, on_device_small(): return result.astype(BF16).reshape(tokens, 1, channels)  1.32 us

profile of v1, /device:TPU:0, one launch (start us, length us, event | category | flops | bytes accessed | tf_op | source)
XLA Modules:
  0.0 20.3 jit_solution(6287891183772653296)
XLA Ops:
  0.0 1.4 %copy.9.w_bias_hbm = bf16[128,4]{1,0:T(8,128)(2,1)} copy(bf16[128,4]{0,1:T(4,128)(2,1)} %param.13) | data formatting | bytes 2048 | tf_op args[5]
  1.4 17.6 %shard_map.82 = f32[32,128]{1,0:T(8,128)} custom-call(bf16[8,4,128]{2,1,0:T(4,128)(2,1)} %pair_hbm.1, s32[8]{0:T(128)} %len_hbm.1, f32[3,128]{1,0:T(4,128)} %gains_hbm.1, bf16[128,640]{1,0:T(8,128)(2,1)} %w_in_hbm.1, bf16[128,128]{1,0:T(8,128)(2,1)} %w_out_hbm.1, bf16[128,4]{1,0:T(8,128)(2,1)} %copy.9.w_bias_hbm, bf16[128,512]{1,0:T(8,128)(2,1)} %w_att_hbm.1, ...), custom_call_target="tpu_custom_call" | custom-call | tf_op jit(solution)/shard_map/pallas_call | solution.py:386
  19.0 1.3 %convert_bitcast_fusion = bf16[32,1,128]{2,0,1:T(8,128)(2,1)} fusion(f32[32,128]{1,0:T(8,128)} %shard_map.82), kind=kLoop, calls=%fused_computation | loop fusion | flops 4096 | bytes 24576 | tf_op jit(solution)/shard_map/reshape | solution.py:413

commit v2 on v1

--- a/solution.py
+++ b/solution.py
@@ -230,7 +230,7 @@
             for d in range(dap_size):
                 to_a = lax.rem(a + d, dap_size)
                 to_s = a * ratio + part
-                remote = pltpu.make_async_remote_copy(
+                remote = lambda part=part, d=d, to_a=to_a, to_s=to_s: pltpu.make_async_remote_copy(
                     src_ref=right_own.at[part],
                     dst_ref=right_buf.at[s],
                     send_sem=right_send.at[part * dap_size + d],
@@ -238,28 +238,28 @@
                     device_id=(to_a, to_s),
                     device_id_type=MESH,
                 )
-                local = None
-                if d == 0:
-                    local = pltpu.make_async_copy(right_own.at[part], right_buf.at[s], right_recv)
-                yield to_s, remote, local
+                yield part, to_s, remote, d == 0
 
     lax.fori_loop(1, slab_size, send_left, 0, unroll=True)
-    for to_s, remote, local in right_copies():
-        if local is None:
-            remote.start()
+    for part, to_s, remote, maybe_self in right_copies():
+        if not maybe_self:
+            remote().start()
         else:
-            pl.when(to_s == s)(local.start)
-            pl.when(to_s != s)(remote.start)
+            own = pltpu.make_async_copy(right_own.at[part], right_buf.at[s], right_recv)
+            pl.when(to_s == s)(own.start)
+            pl.when(to_s != s)(lambda: remote().start())
 
     out_gate = jax.nn.sigmoid(dot(normed_perm, w_in_v[:, 4 * channels :]))
     loads[4].wait()
-    heads = w_bias_hbm.shape[1]
+    heads = w_bias_hbm.shape[0]
     head_dim = channels // heads
     head_shift = head_dim.bit_length() - 1
     spread_row = lax.broadcasted_iota(jnp.int32, (heads, channels), 0)
     spread_lane = lax.broadcasted_iota(jnp.int32, (heads, channels), 1)
     spread = (lax.shift_right_logical(spread_lane, head_shift) == spread_row).astype(F32)
-    w_bias_wide = dot(w_bias_v[...], spread.astype(BF16)).astype(BF16)
+    w_bias_wide = lax.dot_general(
+        w_bias_v[...], spread.astype(BF16), (((0,), (0,)), ((), ())), preferred_element_type=F32
+    ).astype(BF16)
     key_ok = valid(lane & (tokens - 1))
     lane_head = lax.shift_right_logical(lane, head_shift)
     for load in loads[5:]:
@@ -359,14 +359,14 @@
         total = jnp.where(here, jnp.sum(jnp.where(here, weights, 0.0), axis=1, keepdims=True), total)
     weights = (weights / total).astype(BF16)
     gated = (att_gate * dot(weights, value_wide)).astype(BF16)
-    out_ref[...] = columns + dot(gated, w_ao_v[...])
+    out_ref[...] = (columns + dot(gated, w_ao_v[...])).astype(BF16)
 
     pltpu.make_async_copy(others, others, left_send).wait()
-    for to_s, remote, local in right_copies():
-        if local is None:
-            remote.wait_send()
+    for part, to_s, remote, maybe_self in right_copies():
+        if not maybe_self:
+            remote().wait_send()
         else:
-            pl.when(to_s != s)(remote.wait_send)
+            pl.when(to_s != s)(lambda: remote().wait_send())
     for d in range(1, dap_size):
         col_copy(d).wait_send()
     pltpu.make_async_copy(other_rows, other_rows, bias_send).wait()
@@ -374,6 +374,7 @@
 
 def on_device_small(*args):
     pair, chain_lengths = args[:2]
+    args = args[:5] + (args[5].T,) + args[6:]
     rows, cols, channels = pair.shape
     dap_size = lax.axis_size("dap")
     slab_size = lax.axis_size("slab")
@@ -385,7 +386,7 @@
     spaces[1] = pltpu.SMEM
     result = pl.pallas_call(
         functools.partial(small_kernel, dap_size, slab_size, tokens // chain_lengths.shape[0]),
-        out_shape=jax.ShapeDtypeStruct((tokens, channels), F32),
+        out_shape=pltpu.VMEM((tokens, channels), BF16),
         in_specs=[pl.BlockSpec(memory_space=pl.ANY)] * 8,
         out_specs=pl.BlockSpec(memory_space=pltpu.VMEM),
         scratch_shapes=[space(arg.shape, arg.dtype) for space, arg in zip(spaces, args)]
@@ -410,7 +411,7 @@
         ],
         compiler_params=pltpu.CompilerParams(collective_id=0, has_side_effects=True),
     )(*args)
-    return result.astype(BF16).reshape(tokens, 1, channels)
+    return result.reshape(tokens, 1, channels)
 
 
 def fits_small(mesh, shapes):

time: 20.6 us -> 17.8 us (0.86)
  other arithmetic: 1.32 us -> 0 us
  local copies, waits for them, and re-layouts: 1.39 us -> 0.6 us
  Pallas kernels: 17.6 us -> 17 us
    reshape x1 -> x0, other arithmetic: 1.32 us -> none  [on_device_small(): return result.astype(BF16).reshape(tokens, 1, channels)]
    unnamed x1, local copies, waits for them, and re-layouts: 1.39 us -> 0.6 us
    pallas_call x1, Pallas kernels: 17.6 us -> 17 us  [on_device_small(): pl.pallas_call(functools.partial(small_kernel, dap_size, slab_size, token...]
where the time goes in v2:
time: 17.8 us; the launch traced here: 17.6 us
  Pallas kernels  17 us (96%)
  local copies, waits for them, and re-layouts  0.6 us (3%)
    pallas_call x1, Pallas kernels, on_device_small(): pl.pallas_call(functools.partial(small_kernel, dap_size, slab_size, token...  17 us
    unnamed x1, local copies, waits for them, and re-layouts  0.6 us

profile of v2, /device:TPU:0, one launch (start us, length us, event | category | flops | bytes accessed | tf_op | source)
XLA Modules:
  0.0 17.6 jit_solution(15750237582737592131)
XLA Ops:
  0.0 17.0 %shard_map.82 = bf16[32,128]{1,0:T(8,128)(2,1)S(1)} custom-call(bf16[8,4,128]{2,1,0:T(4,128)(2,1)} %pair_hbm.1, s32[8]{0:T(128)} %len_hbm.1, f32[3,128]{1,0:T(4,128)} %gains_hbm.1, bf16[128,640]{1,0:T(8,128)(2,1)} %w_in_hbm.1, bf16[128,128]{1,0:T(8,128)(2,1)} %w_out_hbm.1, bf16[4,128]{1,0:T(4,128)(2,1)} %bitcast.3, bf16[128,512]{1,0:T(8,128)(2,1)} %w_att_hbm.1, ...), custom_call_target="tpu_custom_call" | custom-call | tf_op jit(solution)/shard_map/pallas_call | solution.py:387
  17.0 0.6 %copy.10 = bf16[32,1,128]{2,0,1:T(8,128)(2,1)} copy(bf16[32,1,128]{2,0,1:T(8,128)(2,1)S(1)} %bitcast.2) | data formatting | bytes 16384

commit v3 on v2

--- a/solution.py
+++ b/solution.py
@@ -145,16 +145,24 @@
     s = lax.axis_index("slab")
     me = s * dap_size + a
 
-    def place(index):
-        return (lax.rem(index, dap_size), lax.div(index, dap_size))
+    upper = lax.div(s, slab_size // 2)
+
+    def far_first(n):
+        return upper * n + (1 - upper) * (slab_size - 1 - n)
 
     barrier = pltpu.get_barrier_semaphore()
 
-    def greet(d, carry):
-        pl.semaphore_signal(
-            barrier, inc=1, device_id=place(lax.rem(me + d, devices)), device_id_type=MESH
-        )
-        return carry
+    def greet(to_a, to_s):
+        pl.semaphore_signal(barrier, inc=1, device_id=(to_a, to_s), device_id_type=MESH)
+
+    for n in range(slab_size):
+        for d in range(dap_size):
+            to_s = far_first(n)
+            to_a = lax.rem(a + d, dap_size)
+            if d:
+                greet(to_a, to_s)
+            else:
+                pl.when(to_s != s)(functools.partial(greet, to_a, to_s))
 
     pairs = (
         (pair_hbm, pair_v), (len_hbm, len_s), (gains_hbm, gains_v), (w_in_hbm, w_in_v),
@@ -163,8 +171,6 @@
     loads = [pltpu.make_async_copy(src, dst, in_sem.at[n]) for n, (src, dst) in enumerate(pairs)]
     for load in loads:
         load.start()
-    lax.fori_loop(1, devices, greet, 0, unroll=True)
-
     for load in loads[:4]:
         load.wait()
 
@@ -183,6 +189,12 @@
 
     def norm(values, gain):
         return layer_norm(values, gains_v[gain : gain + 1, :])
+
+    def norm_parts(values, gain):
+        centred = values - jnp.mean(values, axis=-1, keepdims=True)
+        spread = jnp.mean(centred * centred, axis=-1, keepdims=True)
+        scaled = (centred * gains_v[gain : gain + 1, :]).astype(BF16)
+        return scaled, lax.rsqrt(spread + EPSILON)
 
     def dot(x, y):
         return jnp.dot(x, y, preferred_element_type=F32)
@@ -214,16 +226,15 @@
 
     pl.semaphore_wait(barrier, devices - 1)
 
-    def send_left(d, carry):
+    def send_left(to_s):
         pltpu.make_async_remote_copy(
             src_ref=left_buf.at[s],
             dst_ref=left_buf.at[s],
             send_sem=left_send,
             recv_sem=left_recv,
-            device_id=(a, lax.rem(s + d, slab_size)),
+            device_id=(a, to_s),
             device_id_type=MESH,
         ).start()
-        return carry
 
     def right_copies():
         for part in range(ratio):
@@ -240,7 +251,9 @@
                 )
                 yield part, to_s, remote, d == 0
 
-    lax.fori_loop(1, slab_size, send_left, 0, unroll=True)
+    for n in range(slab_size):
+        to_left = far_first(n)
+        pl.when(to_left != s)(functools.partial(send_left, to_left))
     for part, to_s, remote, maybe_self in right_copies():
         if not maybe_self:
             remote().start()
@@ -278,8 +291,9 @@
                 at = k_block * cols * cols + j * cols + k
                 triangle[j] += left_k * right_f32[at : at + 1, :]
     triangle = jnp.concatenate(triangle, axis=0)
-    normed_tri = norm(triangle, 1).astype(BF16)
-    updated = (x_perm + out_gate * dot(normed_tri, w_out_v[...])).astype(BF16).astype(F32)
+    scaled_tri, inverse_tri = norm_parts(triangle, 1)
+    mixed_update = out_gate * inverse_tri * dot(scaled_tri, w_out_v[...])
+    updated = (x_perm + mixed_update).astype(BF16).astype(F32)
     upd_own[...] = updated.reshape(upd_own.shape)
     col_buf[a] = upd_own[a]
 
@@ -294,34 +308,40 @@
             device_id_type=MESH,
         )
 
-    for d in range(1, dap_size):
-        col_copy(d).start()
-
-    normed_local = norm(updated, 2).astype(BF16)
-    bias_all = dot(normed_local, w_bias_wide)
+    scaled_local, inverse_local = norm_parts(updated, 2)
+    bias_all = inverse_local * dot(scaled_local, w_bias_wide)
     bias_row = jnp.sum(
         jnp.where((lane & (block - 1)) == row, bias_all, 0.0), axis=0, keepdims=True
     )
     bias_buf[me] = bias_row.astype(BF16).astype(F32)
 
-    def send_bias(d, carry):
+    def send_bias(to_a, to_s):
         pltpu.make_async_remote_copy(
             src_ref=bias_buf.at[me],
             dst_ref=bias_buf.at[me],
             send_sem=bias_send,
             recv_sem=bias_recv,
-            device_id=place(lax.rem(me + d, devices)),
+            device_id=(to_a, to_s),
             device_id_type=MESH,
         ).start()
-        return carry
-
-    lax.fori_loop(1, devices, send_bias, 0, unroll=True)
+
+    for n in range(slab_size):
+        for d in range(dap_size):
+            to_s = far_first(n)
+            to_a = lax.rem(a + d, dap_size)
+            if d:
+                send_bias(to_a, to_s)
+            else:
+                pl.when(to_s != s)(functools.partial(send_bias, to_a, to_s))
+
+    for d in range(1, dap_size):
+        col_copy(d).start()
 
     other_cols = col_buf.at[pl.ds(0, dap_size - 1)]
     pltpu.make_async_copy(other_cols, other_cols, col_recv).wait()
     columns = col_buf[...].reshape(tokens, channels)
-    normed_cols = norm(columns, 2).astype(BF16)
-    projected = dot(normed_cols, w_att_v[...])
+    scaled_cols, inverse_cols = norm_parts(columns, 2)
+    projected = inverse_cols * dot(scaled_cols, w_att_v[...])
     query = projected[:, :channels].astype(BF16)
     key = projected[:, channels : 2 * channels].astype(BF16)
     value = projected[:, 2 * channels : 3 * channels].astype(BF16)
@@ -329,7 +349,17 @@
     blank = jnp.zeros_like(key)
     key_wide = jnp.concatenate([jnp.where(lane_head == h, key, blank) for h in range(heads)], axis=0)
     value_wide = jnp.concatenate(
-        [jnp.where(lane_head == h, value, blank) for h in range(heads)], axis=0
+        [
+            jnp.concatenate(
+                [
+                    jnp.where(lane_head == h, value, blank),
+                    (lane_head == h).astype(F32).astype(BF16),
+                ],
+                axis=1,
+            )
+            for h in range(heads)
+        ],
+        axis=0,
     )
     scores = lax.dot_general(
         query, key_wide, (((1,), (1,)), ((), ())), preferred_element_type=F32
@@ -352,13 +382,10 @@
         top = jnp.where(
             here, jnp.max(jnp.where(here, scores, -jnp.inf), axis=1, keepdims=True), top
         )
-    weights = jnp.exp(scores - top)
-    total = jnp.zeros_like(scores)
-    for h in range(heads):
-        here = lane_head == h
-        total = jnp.where(here, jnp.sum(jnp.where(here, weights, 0.0), axis=1, keepdims=True), total)
-    weights = (weights / total).astype(BF16)
-    gated = (att_gate * dot(weights, value_wide)).astype(BF16)
+    weights = jnp.exp(scores - top).astype(BF16)
+    summed = dot(weights, value_wide)
+    attended = summed[:, :channels] / summed[:, channels:]
+    gated = (att_gate * attended).astype(BF16)
     out_ref[...] = (columns + dot(gated, w_ao_v[...])).astype(BF16)
 
     pltpu.make_async_copy(others, others, left_send).wait()

time: 17.8 us -> 17.4 us (0.978)
  Pallas kernels: 17 us -> 16.6 us
    pallas_call x1, Pallas kernels: 17 us -> 16.6 us  [on_device_small(): pl.pallas_call(functools.partial(small_kernel, dap_size, slab_size, token...]
where the time goes in v3:
time: 17.4 us; the launch traced here: 17.2 us
  Pallas kernels  16.6 us (95%)
  local copies, waits for them, and re-layouts  0.6 us (3%)
    pallas_call x1, Pallas kernels, on_device_small(): pl.pallas_call(functools.partial(small_kernel, dap_size, slab_size, token...  16.6 us
    unnamed x1, local copies, waits for them, and re-layouts  0.6 us

profile of v3, /device:TPU:0, one launch (start us, length us, event | category | flops | bytes accessed | tf_op | source)
XLA Modules:
  0.0 17.2 jit_solution(2307960009650260364)
XLA Ops:
  0.0 16.6 %shard_map.82 = bf16[32,128]{1,0:T(8,128)(2,1)S(1)} custom-call(bf16[8,4,128]{2,1,0:T(4,128)(2,1)} %pair_hbm.1, s32[8]{0:T(128)} %len_hbm.1, f32[3,128]{1,0:T(4,128)} %gains_hbm.1, bf16[128,640]{1,0:T(8,128)(2,1)} %w_in_hbm.1, bf16[128,128]{1,0:T(8,128)(2,1)} %w_out_hbm.1, bf16[4,128]{1,0:T(4,128)(2,1)} %bitcast.3, bf16[128,512]{1,0:T(8,128)(2,1)} %w_att_hbm.1, ...), custom_call_target="tpu_custom_call" | custom-call | tf_op jit(solution)/shard_map/pallas_call | solution.py:414
  16.6 0.6 %copy.10 = bf16[32,1,128]{2,0,1:T(8,128)(2,1)} copy(bf16[32,1,128]{2,0,1:T(8,128)(2,1)S(1)} %bitcast.2) | data formatting | bytes 16384

commit v4 on v3

--- a/solution.py
+++ b/solution.py
@@ -133,7 +133,7 @@
     out_ref,
     pair_v, len_s, gains_v, w_in_v, w_out_v, w_bias_v, w_att_v, w_ao_v,
     x_scr, left_buf, right_own, right_buf, right_f32, upd_own, col_buf, bias_buf,
-    in_sem, left_send, left_recv, right_send, right_recv,
+    in_sem, left_send, left_recv, right_send, right_recv, share_send, share_recv,
     col_send, col_recv, bias_send, bias_recv,
 ):
     rows, cols, channels = pair_hbm.shape
@@ -236,31 +236,35 @@
             device_id_type=MESH,
         ).start()
 
+    slot = lax.rem(s, 2) * (slab_size // 2) + lax.div(s, 2)
+
     def right_copies():
         for part in range(ratio):
-            for d in range(dap_size):
-                to_a = lax.rem(a + d, dap_size)
+            for d in range(dap_size // 2):
+                to_a = lax.rem(lax.div(a, 2) + d, dap_size // 2) * 2 + lax.rem(s, 2)
                 to_s = a * ratio + part
+                same = jnp.logical_and(to_s == s, to_a == a)
                 remote = lambda part=part, d=d, to_a=to_a, to_s=to_s: pltpu.make_async_remote_copy(
                     src_ref=right_own.at[part],
-                    dst_ref=right_buf.at[s],
-                    send_sem=right_send.at[part * dap_size + d],
+                    dst_ref=right_buf.at[slot],
+                    send_sem=right_send.at[part * (dap_size // 2) + d],
                     recv_sem=right_recv,
                     device_id=(to_a, to_s),
                     device_id_type=MESH,
                 )
-                yield part, to_s, remote, d == 0
+                yield part, same, remote, d == 0
+
+    for part, same, remote, maybe_self in right_copies():
+        if not maybe_self:
+            remote().start()
+        else:
+            own = pltpu.make_async_copy(right_own.at[part], right_buf.at[slot], right_recv)
+            pl.when(same)(own.start)
+            pl.when(jnp.logical_not(same))(lambda: remote().start())
 
     for n in range(slab_size):
         to_left = far_first(n)
         pl.when(to_left != s)(functools.partial(send_left, to_left))
-    for part, to_s, remote, maybe_self in right_copies():
-        if not maybe_self:
-            remote().start()
-        else:
-            own = pltpu.make_async_copy(right_own.at[part], right_buf.at[s], right_recv)
-            pl.when(to_s == s)(own.start)
-            pl.when(to_s != s)(lambda: remote().start())
 
     out_gate = jax.nn.sigmoid(dot(normed_perm, w_in_v[:, 4 * channels :]))
     loads[4].wait()
@@ -278,7 +282,20 @@
     for load in loads[5:]:
         load.wait()
 
-    pltpu.make_async_copy(right_buf, right_buf, right_recv).wait()
+    half = right_buf.at[pl.ds(0, slab_size // 2)]
+    core = lax.rem(a, 2)
+    mine = right_buf.at[pl.ds(core * (slab_size // 2), slab_size // 2)]
+    pltpu.make_async_copy(half, half, right_recv).wait()
+    share = pltpu.make_async_remote_copy(
+        src_ref=mine,
+        dst_ref=mine,
+        send_sem=share_send,
+        recv_sem=share_recv,
+        device_id=(a + 1 - 2 * core, s),
+        device_id_type=MESH,
+    )
+    share.start()
+    share.wait_recv()
     right_f32[...] = right_buf[...].astype(F32).reshape(right_f32.shape)
     others = left_buf.at[pl.ds(0, slab_size - 1)]
     pltpu.make_async_copy(others, others, left_recv).wait()
@@ -288,7 +305,8 @@
         for k in range(cols):
             left_k = left[k * rows : (k + 1) * rows, :]
             for j in range(cols):
-                at = k_block * cols * cols + j * cols + k
+                k_slot = k_block % 2 * (slab_size // 2) + k_block // 2
+                at = k_slot * cols * cols + j * cols + k
                 triangle[j] += left_k * right_f32[at : at + 1, :]
     triangle = jnp.concatenate(triangle, axis=0)
     scaled_tri, inverse_tri = norm_parts(triangle, 1)
@@ -388,12 +406,13 @@
     gated = (att_gate * attended).astype(BF16)
     out_ref[...] = (columns + dot(gated, w_ao_v[...])).astype(BF16)
 
+    share.wait_send()
     pltpu.make_async_copy(others, others, left_send).wait()
-    for part, to_s, remote, maybe_self in right_copies():
+    for part, same, remote, maybe_self in right_copies():
         if not maybe_self:
             remote().wait_send()
         else:
-            pl.when(to_s != s)(lambda: remote().wait_send())
+            pl.when(jnp.logical_not(same))(lambda: remote().wait_send())
     for d in range(1, dap_size):
         col_copy(d).wait_send()
     pltpu.make_async_copy(other_rows, other_rows, bias_send).wait()
@@ -429,7 +448,9 @@
             pltpu.SemaphoreType.DMA((8,)),
             pltpu.SemaphoreType.DMA,
             pltpu.SemaphoreType.DMA,
-            pltpu.SemaphoreType.DMA((ratio * dap_size,)),
+            pltpu.SemaphoreType.DMA((ratio * (dap_size // 2),)),
+            pltpu.SemaphoreType.DMA,
+            pltpu.SemaphoreType.DMA,
             pltpu.SemaphoreType.DMA,
             pltpu.SemaphoreType.DMA((dap_size - 1,)),
             pltpu.SemaphoreType.DMA,

time: 17.4 us -> 17.1 us (0.983)
  Pallas kernels: 16.6 us -> 16.3 us
    pallas_call x1, Pallas kernels: 16.6 us -> 16.3 us  [on_device_small(): pl.pallas_call(functools.partial(small_kernel, dap_size, slab_size, token...]
where the time goes in v4:
time: 17.1 us; the launch traced here: 16.9 us
  Pallas kernels  16.3 us (95%)
  local copies, waits for them, and re-layouts  0.6 us (4%)
    pallas_call x1, Pallas kernels, on_device_small(): pl.pallas_call(functools.partial(small_kernel, dap_size, slab_size, token...  16.3 us
    unnamed x1, local copies, waits for them, and re-layouts  0.6 us

profile of v4, /device:TPU:0, one launch (start us, length us, event | category | flops | bytes accessed | tf_op | source)
XLA Modules:
  0.0 16.9 jit_solution(6742988628843504692)
XLA Ops:
  0.0 16.3 %shard_map.82 = bf16[32,128]{1,0:T(8,128)(2,1)S(1)} custom-call(bf16[8,4,128]{2,1,0:T(4,128)(2,1)} %pair_hbm.1, s32[8]{0:T(128)} %len_hbm.1, f32[3,128]{1,0:T(4,128)} %gains_hbm.1, bf16[128,640]{1,0:T(8,128)(2,1)} %w_in_hbm.1, bf16[128,128]{1,0:T(8,128)(2,1)} %w_out_hbm.1, bf16[4,128]{1,0:T(4,128)(2,1)} %bitcast.3, bf16[128,512]{1,0:T(8,128)(2,1)} %w_att_hbm.1, ...), custom_call_target="tpu_custom_call" | custom-call | tf_op jit(solution)/shard_map/pallas_call | solution.py:433
  16.3 0.6 %copy.10 = bf16[32,1,128]{2,0,1:T(8,128)(2,1)} copy(bf16[32,1,128]{2,0,1:T(8,128)(2,1)S(1)} %bitcast.2) | data formatting | bytes 16384
